TPU v7x, 32 devices: a whole 2x2x4 slice. The times are simulated.
32 devices in a mesh: node: 16 (over z, x, core), group: 2 (over y).
Axes of the slice: x: 2, y: 2, z: 4, core: 2. Of those that a mesh axis runs over, the one named last changes fastest.
Arguments:
- node_feats: bfloat16 [65536, 256], P(('node', 'group')), may hold values from -24 to 24
- w_query: bfloat16 [256, 256], replicated, may hold values from -0.375 to 0.375
- w_key: bfloat16 [256, 256], replicated, may hold values from -0.375 to 0.375
- w_value: bfloat16 [256, 256], replicated, may hold values from -0.375 to 0.375
- w_graph: bfloat16 [256, 256], replicated, may hold values from -0.375 to 0.375
- src_index: int32 [16, 2, 16, 256], P('node', 'group'), may hold values from 0 to 2047
- dst_slot: int32 [16, 2, 16, 256], P('node', 'group'), may hold values from 0 to 2047
- edge_weight: bfloat16 [16, 2, 16, 256], P('node', 'group'), may hold values from 0.049804688 to 0.5
- tile_count: int32 [16, 2, 16], P('node', 'group'), may hold values from 0 to 2, as said below
Outputs:
- layer_out: bfloat16 [65536, 256], P(('node', 'group'))
Inputs may be any that keep to these rules, and one draw needn't show every extreme that they name: `tile_count`: in every group some owner receives 2 tiles from every source device.
All inputs are finite; a program needn't handle non-finite values.
Results may differ from a plain program's by a relative error of at most 0.0047.
Values may be sent and summed in bfloat16 or wider, within the bound.
A program may use at most 64 MiB of HBM per device.

v0:
```python
import jax
import jax.numpy as jnp
from jax import lax
from jax.sharding import PartitionSpec as P

TILE = 128


def add_edges(total, flat_rows, flat_weights, flat_slots):
    total_rows = flat_rows.shape[0]
    block = min(1024, total_rows)
    targets = jnp.arange(total.shape[0], dtype=jnp.int32)

    def accumulate(step, acc):
        part_rows = lax.dynamic_slice_in_dim(flat_rows, step * block, block, 0)
        part_weights = lax.dynamic_slice_in_dim(flat_weights, step * block, block, 0)
        part_slots = lax.dynamic_slice_in_dim(flat_slots, step * block, block, 0)
        table = jnp.where(
            targets[:, None] == part_slots[None, :],
            part_weights[None, :],
            jnp.zeros((), jnp.bfloat16),
        )
        return acc + jnp.dot(table, part_rows, preferred_element_type=jnp.float32)

    return lax.fori_loop(0, total_rows // block, accumulate, total)


def body(
    node_feats, w_query, w_key, w_value, w_graph, src_index, dst_slot, edge_weight, tile_count
):
    owners = lax.axis_size("node")
    rows, width = node_feats.shape
    slot_rows = src_index.shape[3]
    tile_rows = TILE
    sources = src_index.reshape(owners, slot_rows)
    weights = edge_weight.reshape(owners, slot_rows)
    tile_of = jnp.arange(slot_rows, dtype=jnp.int32) // tile_rows
    live = tile_of[None, :] < tile_count.reshape(owners, 1)
    slots = jnp.where(live, dst_slot.reshape(owners, slot_rows), -1)
    outgoing = jnp.take(node_feats, sources.reshape(-1), axis=0).reshape(owners, slot_rows, width)
    start_total = jnp.zeros((rows, width), jnp.float32)
    incoming, in_weights, in_slots = (
        lax.all_to_all(outgoing, "node", split_axis=0, concat_axis=0, tiled=True),
        lax.all_to_all(weights, "node", split_axis=0, concat_axis=0, tiled=True),
        lax.all_to_all(slots, "node", split_axis=0, concat_axis=0, tiled=True),
    )
    phi_q = jax.nn.elu(jnp.dot(node_feats, w_query, preferred_element_type=jnp.float32)) + 1.0
    phi_k = jax.nn.elu(jnp.dot(node_feats, w_key, preferred_element_type=jnp.float32)) + 1.0
    key_b = phi_k.astype(jnp.bfloat16)
    value_b = jnp.dot(node_feats, w_value, preferred_element_type=jnp.float32).astype(jnp.bfloat16)
    kv_local = lax.dot_general(
        key_b, value_b, (((0,), (0,)), ((), ())), preferred_element_type=jnp.float32
    )
    ksum_local = jnp.sum(phi_k, axis=0)
    kv_total, ksum = lax.psum((kv_local, ksum_local), ("node", "group"))
    agg = add_edges(
        start_total, incoming.reshape(-1, width), in_weights.reshape(-1), in_slots.reshape(-1)
    )
    gcn = jnp.dot(agg.astype(jnp.bfloat16), w_graph, preferred_element_type=jnp.float32)
    numer = jnp.dot(phi_q, kv_total, precision=lax.Precision.HIGHEST)
    denom = jnp.dot(phi_q, ksum, precision=lax.Precision.HIGHEST)
    attn = numer / denom[:, None]
    return (0.5 * attn + 0.5 * gcn).astype(jnp.bfloat16)


def solution(mesh):
    in_specs = (
        P(("node", "group"), None),
        P(),
        P(),
        P(),
        P(),
        P("node", "group", None, None),
        P("node", "group", None, None),
        P("node", "group", None, None),
        P("node", "group", None),
    )
    out_specs = P(("node", "group"), None)
    return jax.shard_map(body, mesh=mesh, in_specs=in_specs, out_specs=out_specs, check_vma=False)
```

profile of v0, /device:TPU:0, one launch (start us, length us, event | category | flops | bytes accessed | tf_op | source)
XLA Modules:
  0.0 229.7 jit_solution(374369703517741848)
XLA Ops:
  7.0 1.3 reduce.1
  8.4 0.6 reshape.155
  9.0 7.4 %all-to-all-start.1 = ((bf16[16,2,128]{2,1,0:T(2,128)(2,1)}), bf16[16,2,128]{2,1,0:T(2,128)(2,1)S(1)}, u32[]{:S(2)}, u32[]{:S(2)}) async-start(bf16[16,2,128]{2,1,0:T(2,128)(2,1)} %reshape.155), calls=%async_computation.1 | async-start | bytes 16384 | tf_op jit(solution)/shard_map/all_to_all | solution.py:44
  16.4 0.7 compare_and_fusion
  17.1 0.7 copy.12
  17.9 1.4 compare_select_fusion.5
  19.3 14.6 %gather_fusion = bf16[4096,256]{1,0:T(8,128)(2,1)S(1)} fusion(bf16[2048,256]{1,0:T(8,128)(2,1)S(1)} %copy-done, s32[4096]{0:T(1024)S(1)} %broadcast_clamp_fusion), kind=kCustom, calls=%fused_computation | custom fusion | bytes 4210688 | tf_op jit(solution)/shard_map/jit(_take)/gather | solution.py:40
  33.9 6.0 %all-to-all-start = ((s32[16,1,256]{2,1,0:T(1,128)}), s32[16,1,256]{2,1,0:T(1,128)S(1)}, u32[]{:S(2)}, u32[]{:S(2)}) async-start(s32[16,1,256]{2,1,0:T(1,128)} %compare_select_fusion.5), calls=%async_computation | async-start | bytes 32768 | tf_op jit(solution)/shard_map/all_to_all | solution.py:45
  40.0 1.7 broadcast_select_fusion
  41.6 4.8 %all-to-all-done = s32[16,1,256]{2,1,0:T(1,128)S(1)} async-done(((s32[16,1,256]{2,1,0:T(1,128)}), s32[16,1,256]{2,1,0:T(1,128)S(1)}, u32[]{:S(2)}, u32[]{:S(2)}) %all-to-all-start) | async-done | bytes 16416 | tf_op jit(solution)/shard_map/all_to_all | solution.py:45
  46.5 3.7 %all-to-all-start.2 = ((bf16[16,256,256]{2,1,0:T(8,128)(2,1)}), bf16[16,256,256]{2,1,0:T(8,128)(2,1)S(1)}, u32[]{:S(2)}, u32[]{:S(2)}) async-start(bf16[16,256,256]{2,1,0:T(8,128)(2,1)} %broadcast_select_fusion), calls=%async_computation.2 | async-start | bytes 4194304 | tf_op jit(solution)/shard_map/all_to_all | solution.py:43
  50.2 2.3 %fusion.21 = (f32[256]{0:T(256)S(1)}, f32[2048,256]{1,0:T(8,128)}) fusion(bf16[2048,256]{1,0:T(8,128)(2,1)S(1)} %copy-done, bf16[256,256]{1,0:T(8,128)(2,1)S(1)} %copy-done.4), kind=kOutput, calls=%fused_computation.27 | convolution fusion | flops 271056640 | bytes 3277824 | tf_op jit(solution)/shard_map/dot_general | solution.py:48
  52.6 3.6 %fusion.20 = f32[256,256]{1,0:T(8,128)} fusion(bf16[2048,256]{1,0:T(8,128)(2,1)S(1)} %copy-done, bf16[256,256]{1,0:T(8,128)(2,1)S(1)} %copy-done.5, f32[2048,256]{1,0:T(8,128)} %get-tuple-element.146), kind=kOutput, calls=%fused_computation.26 | convolution fusion | flops 540016640 | bytes 3538944 | tf_op jit(solution)/shard_map/dot_general | solution.py:51
  56.2 64.6 %psum.15 = f32[256]{0:T(256)S(1)} all-reduce(f32[256]{0:T(256)S(1)} %get-tuple-element.145), channel_id=1, replica_groups=mesh['node'=16,'group'=2] {'node','group'}, use_global_device_ids=true, to_apply=%region_2.3 | all-reduce | flops 256 | bytes 2048 | tf_op jit(solution)/shard_map/psum | solution.py:55
  121.2 1.3 copy-done.1
  122.5 2.6 %fusion.23 = f32[1,2048]{1,0:T(1,128)S(1)} fusion(f32[256,1]{0,1:T(1,128)S(1)} %bitcast.36, f32[2048,256]{1,0:T(8,128)S(1)} %fusion.40), kind=kOutput, calls=%fused_computation.29 | convolution fusion | flops 8388608 | bytes 2106368 | tf_op jit(solution)/shard_map/dot_general | solution.py:61
  125.3 73.4 %all-reduce.2.cloned.1.call-done = f32[256,256]{1,0:T(8,128)} async-done(((f32[256,256]{1,0:T(8,128)}), f32[256,256]{1,0:T(8,128)}) %all-reduce.2.cloned.1.call-update) | async-done | bytes 262160 | tf_op jit(solution)/shard_map/psum | solution.py:55
  198.6 5.4 %convolution_divide_fusion = f32[2048,256]{1,0:T(8,128)} fusion(f32[256,256]{1,0:T(8,128)} %all-reduce.2.cloned.1.call-done, f32[2048,256]{1,0:T(8,128)} %copy-done.1, f32[2048]{0:T(1024)S(1)} %bitcast.38), kind=kOutput, calls=%fused_computation.18 | convolution fusion | flops 1613234176 | bytes 4464640 | tf_op jit(solution)/shard_map/dot_general | solution.py:60
  204.0 15.2 %while.14 = (s32[]{:T(128)}, f32[2048,256]{1,0:T(8,128)}, s32[4096]{0:T(1024)S(1)}, bf16[4096]{0:T(1024)(128)(2,1)S(1)}, bf16[4096,256]{1,0:T(8,128)(2,1)S(1)}, ...) while((s32[]{:T(128)}, f32[2048,256]{1,0:T(8,128)}, s32[4096]{0:T(1024)S(1)}, ...), condition=%wide.region_4.5_spmd.clone, body=%wide.region_3.4_spmd.clone.sunk | while | flops 1078984704 | bytes 4737193 | solution.py:25
  204.0 2.6 %fusion.55 = f32[2048,256]{1,0:T(8,128)} fusion(s32[1024]{0:T(1024)S(1)} %dynamic_slice.30, f32[2048,256]{1,0:T(8,128)} %get-tuple-element.188, bf16[1024]{0:T(1024)(128)(2,1)S(1)} %dynamic_slice.31, pred[]{:T(512)S(6)} %compare.7, bf16[4096,256]{1,0:T(8,128)(2,1)S(1)} %get-tuple-element.200, s32[]{:T(128)S(6)} %select_n.134), kind=kOutput, calls=%fused_computation.6.clone.1 | convolution fusion | flops 1078984704 | bytes 4724741 | tf_op jit(solution)/shard_map/while/body/eval_jaxpr/dot_general | solution.py:23
  206.7 4.2 %fusion.55 = f32[2048,256]{1,0:T(8,128)} fusion(s32[1024]{0:T(1024)S(1)} %dynamic_slice.30, f32[2048,256]{1,0:T(8,128)} %get-tuple-element.188, bf16[1024]{0:T(1024)(128)(2,1)S(1)} %dynamic_slice.31, pred[]{:T(512)S(6)} %compare.7, bf16[4096,256]{1,0:T(8,128)(2,1)S(1)} %get-tuple-element.200, s32[]{:T(128)S(6)} %select_n.134), kind=kOutput, calls=%fused_computation.6.clone.1 | convolution fusion | flops 1078984704 | bytes 4724741 | tf_op jit(solution)/shard_map/while/body/eval_jaxpr/dot_general | solution.py:23
  210.8 4.2 %fusion.55 = f32[2048,256]{1,0:T(8,128)} fusion(s32[1024]{0:T(1024)S(1)} %dynamic_slice.30, f32[2048,256]{1,0:T(8,128)} %get-tuple-element.188, bf16[1024]{0:T(1024)(128)(2,1)S(1)} %dynamic_slice.31, pred[]{:T(512)S(6)} %compare.7, bf16[4096,256]{1,0:T(8,128)(2,1)S(1)} %get-tuple-element.200, s32[]{:T(128)S(6)} %select_n.134), kind=kOutput, calls=%fused_computation.6.clone.1 | convolution fusion | flops 1078984704 | bytes 4724741 | tf_op jit(solution)/shard_map/while/body/eval_jaxpr/dot_general | solution.py:23
  215.0 4.2 %fusion.55 = f32[2048,256]{1,0:T(8,128)} fusion(s32[1024]{0:T(1024)S(1)} %dynamic_slice.30, f32[2048,256]{1,0:T(8,128)} %get-tuple-element.188, bf16[1024]{0:T(1024)(128)(2,1)S(1)} %dynamic_slice.31, pred[]{:T(512)S(6)} %compare.7, bf16[4096,256]{1,0:T(8,128)(2,1)S(1)} %get-tuple-element.200, s32[]{:T(128)S(6)} %select_n.134), kind=kOutput, calls=%fused_computation.6.clone.1 | convolution fusion | flops 1078984704 | bytes 4724741 | tf_op jit(solution)/shard_map/while/body/eval_jaxpr/dot_general | solution.py:23
  219.2 3.6 %fusion.15 = bf16[2048,256]{1,0:T(8,128)(2,1)} fusion(f32[2048,256]{1,0:T(8,128)} %convolution_divide_fusion, bf16[256,256]{1,0:T(8,128)(2,1)S(1)} %copy-done.3, f32[2048,256]{1,0:T(8,128)} %get-tuple-element.114), kind=kOutput, calls=%fused_computation.19 | convolution fusion | flops 270532608 | bytes 5373952 | tf_op jit(solution)/shard_map/dot_general | solution.py:59
  (32 shorter events, 1.2 us)
Async XLA Ops:
  6.5 12.8 %copy-start = (bf16[2048,256]{1,0:T(8,128)(2,1)S(1)}, bf16[2048,256]{1,0:T(8,128)(2,1)}, u32[]{:S(2)}) copy-start(bf16[2048,256]{1,0:T(8,128)(2,1)} %param.11) | copy-start | bytes 3145732
  9.0 24.9 %all-to-all-start.1 = ((bf16[16,2,128]{2,1,0:T(2,128)(2,1)}), bf16[16,2,128]{2,1,0:T(2,128)(2,1)S(1)}, u32[]{:S(2)}, u32[]{:S(2)}) async-start(bf16[16,2,128]{2,1,0:T(2,128)(2,1)} %reshape.155), calls=%async_computation.1 | async-start | bytes 16384 | tf_op jit(solution)/shard_map/all_to_all | solution.py:44
  33.9 12.5 %all-to-all-start = ((s32[16,1,256]{2,1,0:T(1,128)}), s32[16,1,256]{2,1,0:T(1,128)S(1)}, u32[]{:S(2)}, u32[]{:S(2)}) async-start(s32[16,1,256]{2,1,0:T(1,128)} %compare_select_fusion.5), calls=%async_computation | async-start | bytes 32768 | tf_op jit(solution)/shard_map/all_to_all | solution.py:45
  41.6 8.6 %copy-start.4 = (bf16[256,256]{1,0:T(8,128)(2,1)S(1)}, bf16[256,256]{1,0:T(8,128)(2,1)}, u32[]{:S(2)}) copy-start(bf16[256,256]{1,0:T(8,128)(2,1)} %param.13) | copy-start | bytes 393220
  46.5 157.6 %all-to-all-start.2 = ((bf16[16,256,256]{2,1,0:T(8,128)(2,1)}), bf16[16,256,256]{2,1,0:T(8,128)(2,1)S(1)}, u32[]{:S(2)}, u32[]{:S(2)}) async-start(bf16[16,256,256]{2,1,0:T(8,128)(2,1)} %broadcast_select_fusion), calls=%async_computation.2 | async-start | bytes 4194304 | tf_op jit(solution)/shard_map/all_to_all | solution.py:43
  50.2 2.4 %copy-start.5 = (bf16[256,256]{1,0:T(8,128)(2,1)S(1)}, bf16[256,256]{1,0:T(8,128)(2,1)}, u32[]{:S(2)}) copy-start(bf16[256,256]{1,0:T(8,128)(2,1)} %param.14) | copy-start | bytes 393220
  50.2 148.5 %all-reduce.2.cloned.1.call-start = ((), (), s32[]{:S(2)}) async-start(), calls=%async_computation.3 | async-start | bytes 524288 | tf_op jit(solution)/shard_map/psum | solution.py:55
  52.6 68.2 %copy-start.2 = (bf16[256,256]{1,0:T(8,128)(2,1)S(1)}, bf16[256,256]{1,0:T(8,128)(2,1)}, u32[]{:S(2)}) copy-start(bf16[256,256]{1,0:T(8,128)(2,1)} %param.12) | copy-start | bytes 393220
  121.2 1.4 copy-start.1
  204.0 15.2 %copy-start.3 = (bf16[256,256]{1,0:T(8,128)(2,1)S(1)}, bf16[256,256]{1,0:T(8,128)(2,1)}, u32[]{:S(2)}) copy-start(bf16[256,256]{1,0:T(8,128)(2,1)} %param.15) | copy-start | bytes 393220
Sparse Core Ops, SparseCore 0:
  56.5 142.0 all-reduce.1
where the time goes:
time: 231 us; the launch traced here: 230 us
  waiting for transfers between devices  78.2 us (34%)
  blocking collectives  64.6 us (28%)
  matrix products  33.2 us (14%)
  local copies, waits for them, and re-layouts  17.9 us (8%)
  starting transfers between devices  17.1 us (7%)
  between operations  13.5 us (6%)
  other arithmetic  5.25 us (2%)
    psum x1, waiting for transfers between devices, body(): kv_total, ksum = lax.psum((kv_local, ksum_local), ('node', 'group'))  73.4 us
    psum x1, blocking collectives, body(): kv_total, ksum = lax.psum((kv_local, ksum_local), ('node', 'group'))  64.6 us
    dot_general x4, matrix products, accumulate(): return acc + jnp.dot(table, part_rows, preferred_element_type=jnp.float32)  15.2 us
    gather x1, local copies, waits for them, and re-layouts, body(): jnp.take(node_feats, sources.reshape(-1), axis=0)  14.6 us
    all_to_all x1, starting transfers between devices, body(): lax.all_to_all(weights, 'node', split_axis=0, concat_axis=0, tiled=True)  7.36 us
    all_to_all x1, starting transfers between devices, body(): lax.all_to_all(slots, 'node', split_axis=0, concat_axis=0, tiled=True)  6.02 us
    dot_general x1, matrix products, body(): numer = jnp.dot(phi_q, kv_total, precision=lax.Precision.HIGHEST)  5.36 us
    all_to_all x1, waiting for transfers between devices, body(): lax.all_to_all(slots, 'node', split_axis=0, concat_axis=0, tiled=True)  4.81 us
  transfers between devices with their start and end apart: 4, of which 2 were waited for; matrix products, arithmetic and copies ran while one was open for 15% of the time, Pallas kernels for 0%

commit v1 on v0

v1 whole, which is shorter than its diff:
```python
import functools

import jax
import jax.numpy as jnp
from jax import lax
from jax.experimental import pallas as pl
from jax.experimental.pallas import tpu as pltpu
from jax.sharding import PartitionSpec as P

TILE = 128
BLK = 256
META = 16
F32 = jnp.float32
BF16 = jnp.bfloat16
MESH = pl.DeviceIdType.MESH


def kernel(
    nodes, groups, reducers, batch,
    feats, w_query, w_key, w_value, w_graph, src_index, dst_slot, edge_weight, tile_count,
    out,
    outgoing, incoming, src_hi, src_lo, acc, q_hi, q_lo, kv_local, kv_parts, kv_total,
    edge_send, edge_recv, part_send, part_recv, total_send, total_recv,
):
    total = nodes * groups
    step = total // reducers
    rows, width = feats.shape
    slots = src_index.shape[3]
    blocks = rows // BLK
    chunk = width // reducers
    node = lax.axis_index("node")
    group = lax.axis_index("group")
    me = node * groups + group
    mine = me // step
    is_reducer = lax.rem(me, step) == 0

    barrier = pltpu.get_barrier_semaphore()

    def greet(j, _):
        peer = lax.rem(me + j, total)
        pl.semaphore_signal(
            barrier, inc=1, device_id=(peer // groups, lax.rem(peer, groups)), device_id_type=MESH
        )
        return 0

    lax.fori_loop(1, total, greet, 0)

    sources = src_index[0, 0]
    spread = (
        lax.broadcasted_iota(jnp.int32, (nodes, nodes * 128), 0)
        == lax.broadcasted_iota(jnp.int32, (nodes, nodes * 128), 1) // 128
    ).astype(F32).astype(BF16)
    for value, ref in ((sources // BLK, src_hi), (lax.rem(sources, BLK), src_lo)):
        columns = jnp.transpose(value.astype(F32)).astype(BF16)
        ref[...] = jnp.dot(columns, spread, preferred_element_type=F32).astype(BF16)

    lanes = lax.broadcasted_iota(jnp.int32, (slots, 128), 1).astype(F32)
    lane_of = (lanes.astype(BF16), (lanes + 128.0).astype(BF16))
    one, zero = jnp.ones((), BF16), jnp.zeros((), BF16)
    tile_of = lax.broadcasted_iota(jnp.int32, (1, slots), 1) // TILE
    meta_row = lax.broadcasted_iota(jnp.int32, (META, slots), 0)

    def pick(owner, put):
        start = pl.multiple_of(owner * 128, 128)
        high = src_hi[:, pl.ds(start, 128)]
        low = src_lo[:, pl.ds(start, 128)]
        picked = jnp.zeros((slots, width), F32)
        for b in range(blocks):
            local = jnp.where(high == jnp.array(b, BF16), low, jnp.array(-1.0, BF16))
            table = jnp.concatenate(
                [jnp.where(local == lane, one, zero) for lane in lane_of], axis=1
            )
            picked += jnp.dot(table, feats[b * BLK:(b + 1) * BLK, :], preferred_element_type=F32)
        put[0:slots, :] = picked.astype(BF16)
        slot = dst_slot[0, 0, pl.ds(owner, 1), :]
        weight = edge_weight[0, 0, pl.ds(owner, 1), :]
        weight = jnp.where(tile_of < tile_count[owner], weight, 0.0)
        meta = jnp.where(meta_row == 0, weight, 0.0)
        meta = jnp.where(meta_row == 1, (slot // BLK).astype(F32), meta)
        meta = jnp.where(meta_row == 2, lax.rem(slot, BLK).astype(F32), meta)
        put[slots:slots + META, :] = meta.astype(BF16)

    pick(node, incoming.at[0])
    pl.semaphore_wait(barrier, total - 1)

    def edge_copy(k):
        return pltpu.make_async_remote_copy(
            src_ref=outgoing.at[k],
            dst_ref=incoming.at[k],
            send_sem=edge_send.at[k],
            recv_sem=edge_recv.at[k],
            device_id=(lax.rem(node + k, nodes), group),
            device_id_type=MESH,
        )

    def send_edges(k, _):
        pick(lax.rem(node + k, nodes), outgoing.at[k])
        edge_copy(k).start()
        return 0

    lax.fori_loop(1, nodes, send_edges, 0)

    key_t = jnp.transpose(w_key[...].astype(F32)).astype(BF16)
    kv = jnp.zeros((width, width), F32)
    ksum = jnp.zeros((width, 1), F32)

    def phi(x):
        return jnp.where(x > 0.0, x + 1.0, jnp.exp(jnp.minimum(x, 0.0)))

    part = min(512, rows)

    def project(b, carry):
        kv, ksum = carry
        at = pl.ds(pl.multiple_of(b * part, part), part)
        x = feats[at, :]
        q = phi(jnp.dot(x, w_query[...], preferred_element_type=F32))
        high = q.astype(BF16)
        q_hi[at, :] = high
        q_lo[at, :] = (q - high.astype(F32)).astype(BF16)
        k = phi(lax.dot_general(key_t, x, (((1,), (1,)), ((), ())), preferred_element_type=F32))
        v = jnp.dot(x, w_value[...], preferred_element_type=F32).astype(BF16)
        kv = kv + jnp.dot(k.astype(BF16), v, preferred_element_type=F32)
        return kv, ksum + jnp.sum(k, axis=1, keepdims=True)

    kv, ksum = lax.fori_loop(0, rows // part, project, (kv, ksum))
    kv_local[:, :, 0:width] = kv.reshape(reducers, chunk, width)
    kv_local[:, :, width:] = jnp.broadcast_to(ksum, (width, 128)).reshape(reducers, chunk, 128)

    def part_copy(j):
        c = lax.rem(mine + j, reducers)
        peer = c * step
        return pltpu.make_async_remote_copy(
            src_ref=kv_local.at[c],
            dst_ref=kv_parts.at[lax.rem(me - peer - 1 + total, total)],
            send_sem=part_send.at[j],
            recv_sem=part_recv,
            device_id=(peer // groups, lax.rem(peer, groups)),
            device_id_type=MESH,
        )

    def each_part(act):
        if step > 1:
            @pl.when(jnp.logical_not(is_reducer))
            def _():
                act(part_copy(0))

        def go(j, _):
            act(part_copy(j))
            return 0

        lax.fori_loop(1, reducers, go, 0)

    each_part(lambda copy: copy.start())

    row_of = lax.broadcasted_iota(jnp.int32, (BLK, slots), 0).astype(F32).astype(BF16)

    def add_batch(first, fresh):
        weights, highs, lows = [], [], []
        for i in range(batch):
            meta = incoming[first + i, slots:slots + META, :]
            weights.append(meta[0:1, :])
            highs.append(meta[1:2, :])
            lows.append(meta[2:3, :])

        def one_block(b, _):
            at = pl.ds(pl.multiple_of(b * BLK, BLK), BLK)
            here = lax.convert_element_type(b, F32)
            sums = jnp.zeros((BLK, width), F32) if fresh else acc[at, :]
            for i in range(batch):
                local = jnp.where(highs[i].astype(F32) == here, lows[i].astype(F32), -1.0).astype(BF16)
                table = jnp.where(row_of == local, weights[i], zero)
                sums += jnp.dot(table, incoming[first + i, 0:slots, :], preferred_element_type=F32)
            acc[at, :] = sums
            return 0

        lax.fori_loop(0, blocks, one_block, 0)

    for i in range(1, batch):
        edge_copy(i).wait_recv()
    add_batch(0, True)

    def total_copy(j):
        peer = lax.rem(me + j, total)
        return pltpu.make_async_remote_copy(
            src_ref=kv_total.at[mine],
            dst_ref=kv_total.at[mine],
            send_sem=total_send,
            recv_sem=total_recv,
            device_id=(peer // groups, lax.rem(peer, groups)),
            device_id_type=MESH,
        )

    @pl.when(is_reducer)
    def _():
        pltpu.make_async_copy(kv_parts, kv_parts, part_recv).wait()
        kv_total[mine] = kv_local[mine] + jnp.sum(kv_parts[...], axis=0)

        def go(j, _):
            total_copy(j).start()
            return 0

        lax.fori_loop(1, total, go, 0)

    def rest(g, _):
        first = g * batch
        for i in range(batch):
            edge_copy(first + i).wait_recv()
        add_batch(first, False)
        return 0

    lax.fori_loop(1, nodes // batch, rest, 0)

    others = kv_total.at[pl.ds(0, reducers - 1)]
    if step > 1:
        @pl.when(is_reducer)
        def _():
            pltpu.make_async_copy(others, others, total_recv).wait()

        @pl.when(jnp.logical_not(is_reducer))
        def _():
            pltpu.make_async_copy(kv_total, kv_total, total_recv).wait()
    else:
        pltpu.make_async_copy(others, others, total_recv).wait()

    summary = kv_total[...].reshape(width, width + 128)
    s_hi = summary.astype(BF16)
    s_lo = (summary - s_hi.astype(F32)).astype(BF16)

    def finish(b, _):
        at = pl.ds(pl.multiple_of(b * BLK, BLK), BLK)
        gcn = jnp.dot(acc[at, :].astype(BF16), w_graph[...], preferred_element_type=F32)
        high, low = q_hi[at, :], q_lo[at, :]
        both = jnp.dot(high, s_hi, preferred_element_type=F32)
        both += jnp.dot(high, s_lo, preferred_element_type=F32)
        both += jnp.dot(low, s_hi, preferred_element_type=F32)
        under = 1.0 / both[:, width:]
        attn = both[:, 0:width] * jnp.concatenate([under] * (width // 128), axis=1)
        out[at, :] = (0.5 * attn + 0.5 * gcn).astype(BF16)
        return 0

    lax.fori_loop(0, blocks, finish, 0)

    def sent(k, _):
        edge_copy(k).wait_send()
        return 0

    lax.fori_loop(1, nodes, sent, 0)
    each_part(lambda copy: copy.wait_send())

    @pl.when(is_reducer)
    def _():
        pltpu.make_async_copy(kv_parts, kv_parts, total_send).wait()


def body(nodes, groups, *arrays):
    feats, src_index = arrays[0], arrays[5]
    rows, width = feats.shape
    slots = src_index.shape[3]
    total = nodes * groups
    reducers = min(total, width // 8)
    batch = 4
    edges = arrays[7].astype(F32)
    counts = arrays[8].reshape(-1)
    vmem = pl.BlockSpec(memory_space=pltpu.VMEM)
    return pl.pallas_call(
        functools.partial(kernel, nodes, groups, reducers, batch),
        out_shape=jax.ShapeDtypeStruct((rows, width), BF16),
        in_specs=[vmem] * 8 + [pl.BlockSpec(memory_space=pltpu.SMEM)],
        out_specs=vmem,
        scratch_shapes=[
            pltpu.VMEM((nodes, slots + META, width), BF16),
            pltpu.VMEM((nodes, slots + META, width), BF16),
            pltpu.VMEM((slots, nodes * 128), BF16),
            pltpu.VMEM((slots, nodes * 128), BF16),
            pltpu.VMEM((rows, width), F32),
            pltpu.VMEM((rows, width), BF16),
            pltpu.VMEM((rows, width), BF16),
            pltpu.VMEM((reducers, width // reducers, width + 128), F32),
            pltpu.VMEM((total - 1, width // reducers, width + 128), F32),
            pltpu.VMEM((reducers, width // reducers, width + 128), F32),
            pltpu.SemaphoreType.DMA((nodes,)),
            pltpu.SemaphoreType.DMA((nodes,)),
            pltpu.SemaphoreType.DMA((reducers,)),
            pltpu.SemaphoreType.DMA,
            pltpu.SemaphoreType.DMA,
            pltpu.SemaphoreType.DMA,
        ],
        compiler_params=pltpu.CompilerParams(
            collective_id=0, has_side_effects=True, vmem_limit_bytes=48 * 1024 * 1024
        ),
    )(*arrays[:7], edges, counts)


def solution(mesh):
    in_specs = (
        P(("node", "group"), None),
        P(),
        P(),
        P(),
        P(),
        P("node", "group", None, None),
        P("node", "group", None, None),
        P("node", "group", None, None),
        P("node", "group", None),
    )
    return jax.shard_map(
        functools.partial(body, mesh.shape["node"], mesh.shape["group"]),
        mesh=mesh,
        in_specs=in_specs,
        out_specs=P(("node", "group"), None),
        check_vma=False,
    )
```

time: 231 us -> 87.4 us (0.38)
  the two profiles are of different devices: /device:TPU:0 before, /device:TPU:27 now
where the time goes in v1:
time: 87.4 us; the launch traced here: 87 us
  Pallas kernels  79.7 us (91%)
  local copies, waits for them, and re-layouts  6.53 us (7%)
    pallas_call x1, Pallas kernels, body(): pl.pallas_call(functools.partial(kernel, nodes, groups, reducers, batch),...  79.7 us
    unnamed x17, local copies, waits for them, and re-layouts  6.53 us

profile of v1, /device:TPU:27, one launch (start us, length us, event | category | flops | bytes accessed | tf_op | source)
XLA Modules:
  0.0 87.0 jit_solution(17959405532028142236)
XLA Ops:
  0.0 0.0 copy-start.5
  0.0 0.0 copy-start.7
  0.0 0.7 convert_element_type.3.edge_weight
  0.7 0.0 copy-done.5
  0.7 0.0 copy-done.7
  0.7 0.0 copy-start
  0.7 1.2 %copy-done = bf16[2048,256]{1,0:T(8,128)(2,1)S(1)} copy-done((bf16[2048,256]{1,0:T(8,128)(2,1)S(1)}, bf16[2048,256]{1,0:T(8,128)(2,1)}, u32[]{:S(2)}) %copy-start) | copy-done | bytes 1048600
  2.0 0.0 copy-start.1
  2.0 0.9 %copy-done.1 = bf16[256,256]{1,0:T(8,128)(2,1)S(1)} copy-done((bf16[256,256]{1,0:T(8,128)(2,1)S(1)}, bf16[256,256]{1,0:T(8,128)(2,1)}, u32[]{:S(2)}) %copy-start.1) | copy-done | bytes 131096
  2.9 0.0 copy-start.2
  2.9 0.9 %copy-done.2 = bf16[256,256]{1,0:T(8,128)(2,1)S(1)} copy-done((bf16[256,256]{1,0:T(8,128)(2,1)S(1)}, bf16[256,256]{1,0:T(8,128)(2,1)}, u32[]{:S(2)}) %copy-start.2) | copy-done | bytes 131096
  3.8 0.0 copy-start.3
  3.8 0.9 %copy-done.3 = bf16[256,256]{1,0:T(8,128)(2,1)S(1)} copy-done((bf16[256,256]{1,0:T(8,128)(2,1)S(1)}, bf16[256,256]{1,0:T(8,128)(2,1)}, u32[]{:S(2)}) %copy-start.3) | copy-done | bytes 131096
  4.7 0.0 copy-start.4
  4.7 0.9 %copy-done.4 = bf16[256,256]{1,0:T(8,128)(2,1)S(1)} copy-done((bf16[256,256]{1,0:T(8,128)(2,1)S(1)}, bf16[256,256]{1,0:T(8,128)(2,1)}, u32[]{:S(2)}) %copy-start.4) | copy-done | bytes 131096
  5.6 0.0 copy-start.6
  5.6 0.7 copy-done.6
  6.3 79.7 %shard_map.91 = bf16[2048,256]{1,0:T(8,128)(2,1)S(1)} custom-call(bf16[2048,256]{1,0:T(8,128)(2,1)S(1)} %copy-done, bf16[256,256]{1,0:T(8,128)(2,1)S(1)} %copy-done.1, bf16[256,256]{1,0:T(8,128)(2,1)S(1)} %copy-done.2, bf16[256,256]{1,0:T(8,128)(2,1)S(1)} %copy-done.3, bf16[256,256]{1,0:T(8,128)(2,1)S(1)} %copy-done.4, s32[1,1,16,256]{3,2,1,0:T(8,128)S(1)} %copy-done.5, ...), custom_call_target="tpu_custom_call" | custom-call | tf_op jit(solution)/shard_map/pallas_call | solution.py:265
  86.0 1.0 %copy.11 = bf16[2048,256]{1,0:T(8,128)(2,1)} copy(bf16[2048,256]{1,0:T(8,128)(2,1)S(1)} %shard_map.91) | data formatting | bytes 2097152
Async XLA Ops:
  0.0 0.7 copy-start.5
  0.0 0.7 copy-start.7
  0.7 1.2 %copy-start = (bf16[2048,256]{1,0:T(8,128)(2,1)S(1)}, bf16[2048,256]{1,0:T(8,128)(2,1)}, u32[]{:S(2)}) copy-start(bf16[2048,256]{1,0:T(8,128)(2,1)} %feats.1) | copy-start | bytes 3145732
  2.0 0.9 %copy-start.1 = (bf16[256,256]{1,0:T(8,128)(2,1)S(1)}, bf16[256,256]{1,0:T(8,128)(2,1)}, u32[]{:S(2)}) copy-start(bf16[256,256]{1,0:T(8,128)(2,1)} %w_query.1) | copy-start | bytes 393220
  2.9 0.9 %copy-start.2 = (bf16[256,256]{1,0:T(8,128)(2,1)S(1)}, bf16[256,256]{1,0:T(8,128)(2,1)}, u32[]{:S(2)}) copy-start(bf16[256,256]{1,0:T(8,128)(2,1)} %w_key.1) | copy-start | bytes 393220
  3.8 0.9 %copy-start.3 = (bf16[256,256]{1,0:T(8,128)(2,1)S(1)}, bf16[256,256]{1,0:T(8,128)(2,1)}, u32[]{:S(2)}) copy-start(bf16[256,256]{1,0:T(8,128)(2,1)} %w_value.1) | copy-start | bytes 393220
  4.7 0.9 %copy-start.4 = (bf16[256,256]{1,0:T(8,128)(2,1)S(1)}, bf16[256,256]{1,0:T(8,128)(2,1)}, u32[]{:S(2)}) copy-start(bf16[256,256]{1,0:T(8,128)(2,1)} %w_graph.1) | copy-start | bytes 393220
  5.6 0.7 copy-start.6

commit v2 on v1

v2 whole, which is shorter than its diff:
```python
import functools

import jax
import jax.numpy as jnp
from jax import lax
from jax.experimental import pallas as pl
from jax.experimental.pallas import tpu as pltpu
from jax.sharding import PartitionSpec as P

TILE = 128
BLK = 256
META = 16
F32 = jnp.float32
BF16 = jnp.bfloat16
MESH = pl.DeviceIdType.MESH


def kernel(
    nodes, groups, inner, batch,
    feats_in, w_query_in, w_key_in, w_value_in, w_graph_in, src_in, dst_in, weight_in, count_in,
    out,
    feats, w_query, w_key, w_value, w_graph, src_index, dst_slot, edge_weight, tile_count, live_weight,
    outgoing, incoming, src_hi, src_lo, acc, attn, q_hi, q_lo,
    kv_local, kv_parts, kv_plane, kv_columns, kv_total,
    load_sem, edge_send, edge_recv, part_send, part_recv, column_send, column_recv, total_send, total_recv,
):
    total = nodes * groups
    plane = inner * groups
    outer = nodes // inner
    rows, width = feats.shape
    slots = src_index.shape[3]
    blocks = rows // BLK
    chunk = width // plane
    node = lax.axis_index("node")
    group = lax.axis_index("group")
    me = node * groups + group
    level = node // inner
    spot = lax.rem(node, inner) * groups + group

    loads = [
        pltpu.make_async_copy(src, dst, load_sem.at[i])
        for i, (src, dst) in enumerate((
            (src_in, src_index), (count_in, tile_count), (dst_in, dst_slot), (weight_in, edge_weight),
            (feats_in, feats), (w_query_in, w_query), (w_key_in, w_key), (w_value_in, w_value),
            (w_graph_in, w_graph),
        ))
    ]
    for load in loads:
        load.start()
    barrier = pltpu.get_barrier_semaphore()

    def greet(j, _):
        peer = lax.rem(me + j, total)
        pl.semaphore_signal(
            barrier, inc=1, device_id=(peer // groups, lax.rem(peer, groups)), device_id_type=MESH
        )
        return 0

    lax.fori_loop(1, total, greet, 0)
    for load in loads[0:4]:
        load.wait()

    sources = src_index[0, 0]
    spread = (
        lax.broadcasted_iota(jnp.int32, (nodes, nodes * 128), 0)
        == lax.broadcasted_iota(jnp.int32, (nodes, nodes * 128), 1) // 128
    ).astype(F32).astype(BF16)
    for value, ref in ((sources // BLK, src_hi), (lax.rem(sources, BLK), src_lo)):
        columns = jnp.transpose(value.astype(F32)).astype(BF16)
        ref[...] = jnp.dot(columns, spread, preferred_element_type=F32).astype(BF16)

    lanes = lax.broadcasted_iota(jnp.int32, (slots, 128), 1).astype(F32)
    lane_of = (lanes.astype(BF16), (lanes + 128.0).astype(BF16))
    one, zero = jnp.ones((), BF16), jnp.zeros((), BF16)
    tile_of = (lax.broadcasted_iota(jnp.int32, (nodes, slots), 1) // TILE).astype(F32)
    diagonal = lax.broadcasted_iota(jnp.int32, (nodes, nodes), 0) == lax.broadcasted_iota(
        jnp.int32, (nodes, nodes), 1
    )
    counts = jnp.sum(
        jnp.where(diagonal, tile_count[0].astype(F32), 0.0), axis=1, keepdims=True
    )
    live_weight[...] = jnp.where(tile_of < counts, edge_weight[0, 0].astype(F32), 0.0)
    meta_row = lax.broadcasted_iota(jnp.int32, (META, slots), 0)

    def pick(owner, put):
        start = pl.multiple_of(owner * 128, 128)
        high = src_hi[:, pl.ds(start, 128)]
        low = src_lo[:, pl.ds(start, 128)]
        picked = jnp.zeros((slots, width), F32)
        for b in range(blocks):
            local = jnp.where(high == jnp.array(b, BF16), low, jnp.array(-1.0, BF16))
            table = jnp.concatenate(
                [jnp.where(local == lane, one, zero) for lane in lane_of], axis=1
            )
            picked += jnp.dot(table, feats[b * BLK:(b + 1) * BLK, :], preferred_element_type=F32)
        put[0:slots, :] = picked.astype(BF16)
        slot = dst_slot[0, 0, pl.ds(owner, 1), :]
        weight = live_weight[pl.ds(owner, 1), :]
        meta = jnp.where(meta_row == 0, weight, 0.0)
        meta = jnp.where(meta_row == 1, (slot // BLK).astype(F32), meta)
        meta = jnp.where(meta_row == 2, lax.rem(slot, BLK).astype(F32), meta)
        put[slots:slots + META, :] = meta.astype(BF16)

    def edge_copy(k):
        return pltpu.make_async_remote_copy(
            src_ref=outgoing.at[k],
            dst_ref=incoming.at[k],
            send_sem=edge_send.at[k],
            recv_sem=edge_recv.at[k],
            device_id=(lax.rem(node + k, nodes), group),
            device_id_type=MESH,
        )

    def send_edges(k, _):
        pick(lax.rem(node + k, nodes), outgoing.at[k])
        edge_copy(k).start()
        return 0


    def phi(x):
        return jnp.where(x > 0.0, x + 1.0, jnp.exp(jnp.minimum(x, 0.0)))

    part = min(512, rows)

    def project(b, carry):
        kv, ksum = carry
        at = pl.ds(pl.multiple_of(b * part, part), part)
        x = feats[at, :]
        q = phi(jnp.dot(x, w_query[...], preferred_element_type=F32))
        high = q.astype(BF16)
        q_hi[at, :] = high
        q_lo[at, :] = (q - high.astype(F32)).astype(BF16)
        key_t = jnp.transpose(w_key[...].astype(F32)).astype(BF16)
        k = phi(lax.dot_general(key_t, x, (((1,), (1,)), ((), ())), preferred_element_type=F32))
        v = jnp.dot(x, w_value[...], preferred_element_type=F32).astype(BF16)
        kv = kv + jnp.dot(k.astype(BF16), v, preferred_element_type=F32)
        return kv, ksum + jnp.sum(k, axis=1, keepdims=True)

    def summarize():
        kv = jnp.zeros((width, width), F32)
        ksum = jnp.zeros((width, 1), F32)
        kv, ksum = lax.fori_loop(0, rows // part, project, (kv, ksum))
        kv_local[:, :, 0:width] = kv.reshape(plane, chunk, width)
        kv_local[:, :, width:] = jnp.broadcast_to(ksum, (width, 128)).reshape(plane, chunk, 128)

    def place(j):
        peer = lax.rem(spot + j, plane)
        return peer, (level * inner + peer // groups, lax.rem(peer, groups))

    def part_copy(j):
        peer, device = place(j)
        return pltpu.make_async_remote_copy(
            src_ref=kv_local.at[peer], dst_ref=kv_parts.at[j - 1],
            send_sem=part_send.at[j], recv_sem=part_recv.at[j],
            device_id=device, device_id_type=MESH,
        )

    def column_copy(j):
        return pltpu.make_async_remote_copy(
            src_ref=kv_plane, dst_ref=kv_columns.at[j - 1],
            send_sem=column_send.at[j], recv_sem=column_recv.at[j],
            device_id=(lax.rem(node + j * inner, nodes), group), device_id_type=MESH,
        )

    def total_copy(j):
        peer, device = place(j)
        return pltpu.make_async_remote_copy(
            src_ref=kv_total.at[spot], dst_ref=kv_total.at[spot],
            send_sem=total_send.at[j], recv_sem=total_recv,
            device_id=device, device_id_type=MESH,
        )

    def each(first, last, act):
        def go(j, _):
            act(j)
            return 0

        lax.fori_loop(first, last, go, 0)

    def start_parts():
        each(1, plane, lambda j: part_copy(j).start())

    def start_columns():
        each(1, plane, lambda j: part_copy(j).wait_recv())
        kv_plane[...] = kv_local[spot] + jnp.sum(kv_parts[...], axis=0)
        each(1, outer, lambda j: column_copy(j).start())

    def start_totals():
        each(1, outer, lambda j: column_copy(j).wait_recv())
        kv_total[spot] = kv_plane[...] + jnp.sum(kv_columns[...], axis=0)
        each(1, plane, lambda j: total_copy(j).start())

    def wait_totals():
        others = kv_total.at[pl.ds(0, plane - 1)]
        pltpu.make_async_copy(others, others, total_recv).wait()

    row_of = lax.broadcasted_iota(jnp.int32, (BLK, slots), 0).astype(F32).astype(BF16)

    def add_batch(first, fresh, last=False):
        weights, highs, lows = [], [], []
        for i in range(batch):
            meta = incoming[first + i, slots:slots + META, :]
            weights.append(meta[0:1, :])
            highs.append(meta[1:2, :])
            lows.append(meta[2:3, :])
        arrived = jnp.concatenate([incoming[first + i, 0:slots, :] for i in range(batch)], axis=0)

        def one_block(b, _):
            at = pl.ds(pl.multiple_of(b * BLK, BLK), BLK)
            here = lax.convert_element_type(b, F32)
            tables = []
            for i in range(batch):
                local = jnp.where(highs[i].astype(F32) == here, lows[i].astype(F32), -1.0).astype(BF16)
                tables.append(jnp.where(row_of == local, weights[i], zero))
            sums = jnp.dot(jnp.concatenate(tables, axis=1), arrived, preferred_element_type=F32)
            if last:
                agg = (acc[at, :] + sums).astype(BF16)
                gcn = jnp.dot(agg, w_graph[...], preferred_element_type=F32)
                out[at, :] = (attn[at, :] + 0.5 * gcn).astype(BF16)
            else:
                acc[at, :] = sums if fresh else acc[at, :] + sums
            return 0

        lax.fori_loop(0, blocks, one_block, 0)

    def first_batch():
        for i in range(1, batch):
            edge_copy(i).wait_recv()
        add_batch(0, True)

    def rest(g, _):
        first = g * batch
        for i in range(batch):
            edge_copy(first + i).wait_recv()
        add_batch(first, False)
        return 0

    def attend():
        summary = kv_total[...].reshape(width, width + 128)
        s_hi = summary.astype(BF16)
        s_lo = (summary - s_hi.astype(F32)).astype(BF16)

        def one_block(b, _):
            at = pl.ds(pl.multiple_of(b * BLK, BLK), BLK)
            high, low = q_hi[at, :], q_lo[at, :]
            both = jnp.dot(high, s_hi, preferred_element_type=F32)
            both += jnp.dot(high, s_lo, preferred_element_type=F32)
            both += jnp.dot(low, s_hi, preferred_element_type=F32)
            under = 0.5 / both[:, width:]
            attn[at, :] = both[:, 0:width] * jnp.concatenate([under] * (width // 128), axis=1)
            return 0

        lax.fori_loop(0, blocks, one_block, 0)

    loads[4].wait()
    pl.semaphore_wait(barrier, total - 1)
    lax.fori_loop(1, nodes, send_edges, 0)
    for load in loads[5:]:
        load.wait()
    summarize()
    start_parts()
    pick(node, incoming.at[0])
    start_columns()
    first_batch()
    start_totals()
    lax.fori_loop(1, nodes // batch - 1, rest, 0)
    wait_totals()
    attend()
    last = nodes - batch
    for i in range(batch):
        edge_copy(last + i).wait_recv()
    add_batch(last, False, True)

    def sent(k, _):
        edge_copy(k).wait_send()
        return 0

    lax.fori_loop(1, nodes, sent, 0)
    each(1, plane, lambda j: part_copy(j).wait_send())
    each(1, outer, lambda j: column_copy(j).wait_send())
    each(1, plane, lambda j: total_copy(j).wait_send())


def body(nodes, groups, *arrays):
    feats, src_index = arrays[0], arrays[5]
    rows, width = feats.shape
    slots = src_index.shape[3]
    inner = 4
    plane = inner * groups
    chunk = (width // plane, width + 128)
    hbm = pl.BlockSpec(memory_space=pltpu.HBM)
    return pl.pallas_call(
        functools.partial(kernel, nodes, groups, inner, 4),
        out_shape=jax.ShapeDtypeStruct((rows, width), BF16),
        in_specs=[hbm] * 9,
        out_specs=pl.BlockSpec(memory_space=pltpu.VMEM),
        scratch_shapes=[pltpu.VMEM(a.shape, a.dtype) for a in arrays] + [
            pltpu.VMEM((nodes, slots), F32),
            pltpu.VMEM((nodes, slots + META, width), BF16),
            pltpu.VMEM((nodes, slots + META, width), BF16),
            pltpu.VMEM((slots, nodes * 128), BF16),
            pltpu.VMEM((slots, nodes * 128), BF16),
            pltpu.VMEM((rows, width), F32),
            pltpu.VMEM((rows, width), F32),
            pltpu.VMEM((rows, width), BF16),
            pltpu.VMEM((rows, width), BF16),
            pltpu.VMEM((plane, *chunk), F32),
            pltpu.VMEM((plane - 1, *chunk), F32),
            pltpu.VMEM(chunk, F32),
            pltpu.VMEM((nodes // inner - 1, *chunk), F32),
            pltpu.VMEM((plane, *chunk), F32),
            pltpu.SemaphoreType.DMA((len(arrays),)),
            pltpu.SemaphoreType.DMA((nodes,)),
            pltpu.SemaphoreType.DMA((nodes,)),
            pltpu.SemaphoreType.DMA((plane,)),
            pltpu.SemaphoreType.DMA((plane,)),
            pltpu.SemaphoreType.DMA((nodes // inner,)),
            pltpu.SemaphoreType.DMA((nodes // inner,)),
            pltpu.SemaphoreType.DMA((plane,)),
            pltpu.SemaphoreType.DMA,
        ],
        compiler_params=pltpu.CompilerParams(
            collective_id=0, has_side_effects=True, vmem_limit_bytes=62 * 1024 * 1024
        ),
    )(*arrays)


def solution(mesh):
    in_specs = (
        P(("node", "group"), None),
        P(),
        P(),
        P(),
        P(),
        P("node", "group", None, None),
        P("node", "group", None, None),
        P("node", "group", None, None),
        P("node", "group", None),
    )
    return jax.shard_map(
        functools.partial(body, mesh.shape["node"], mesh.shape["group"]),
        mesh=mesh,
        in_specs=in_specs,
        out_specs=P(("node", "group"), None),
        check_vma=False,
    )
```

time: 87.4 us -> 77.8 us (0.89)
  the two profiles are of different devices: /device:TPU:27 before, /device:TPU:0 now
where the time goes in v2:
time: 77.8 us; the launch traced here: 77.6 us
  Pallas kernels  75.3 us (97%)
  local copies, waits for them, and re-layouts  2.26 us (3%)
    pallas_call x1, Pallas kernels, body(): pl.pallas_call(functools.partial(kernel, nodes, groups, inner, 4), out_sh...  75.3 us
    unnamed x1, local copies, waits for them, and re-layouts  2.26 us

profile of v2, /device:TPU:0, one launch (start us, length us, event | category | flops | bytes accessed | tf_op | source)
XLA Modules:
  0.0 77.6 jit_solution(5851632023781448272)
XLA Ops:
  0.0 75.3 %shard_map.91 = bf16[2048,256]{1,0:T(8,128)(2,1)} custom-call(bf16[2048,256]{1,0:T(8,128)(2,1)} %feats_in.1, bf16[256,256]{1,0:T(8,128)(2,1)} %w_query_in.1, bf16[256,256]{1,0:T(8,128)(2,1)} %w_key_in.1, bf16[256,256]{1,0:T(8,128)(2,1)} %w_value_in.1, bf16[256,256]{1,0:T(8,128)(2,1)} %w_graph_in.1, s32[1,1,16,256]{3,2,1,0:T(8,128)} %src_in.1, ...), custom_call_target="tpu_custom_call" | custom-call | tf_op jit(solution)/shard_map/pallas_call | solution.py:292
  75.3 2.3 %copy.11 = bf16[2048,256]{1,0:T(8,128)(2,1)} copy(bf16[2048,256]{1,0:T(8,128)(2,1)} %shard_map.91) | data formatting | bytes 2097152

commit v3 on v2

--- a/solution.py
+++ b/solution.py
@@ -254,15 +254,18 @@
 
     loads[4].wait()
     pl.semaphore_wait(barrier, total - 1)
-    lax.fori_loop(1, nodes, send_edges, 0)
+    lax.fori_loop(1, 5, send_edges, 0)
     for load in loads[5:]:
         load.wait()
     summarize()
     start_parts()
+    lax.fori_loop(5, 8, send_edges, 0)
+    start_columns()
+    lax.fori_loop(8, 12, send_edges, 0)
+    start_totals()
+    lax.fori_loop(12, nodes, send_edges, 0)
     pick(node, incoming.at[0])
-    start_columns()
     first_batch()
-    start_totals()
     lax.fori_loop(1, nodes // batch - 1, rest, 0)
     wait_totals()
     attend()

time: 77.8 us -> 75 us (0.964)
  the two profiles are of different devices: /device:TPU:0 before, /device:TPU:27 now
where the time goes in v3:
time: 75 us; the launch traced here: 74.8 us
  Pallas kernels  72.5 us (97%)
  local copies, waits for them, and re-layouts  2.26 us (3%)
    pallas_call x1, Pallas kernels, body(): pl.pallas_call(functools.partial(kernel, nodes, groups, inner, 4), out_sh...  72.5 us
    unnamed x1, local copies, waits for them, and re-layouts  2.26 us

profile of v3, /device:TPU:27, one launch (start us, length us, event | category | flops | bytes accessed | tf_op | source)
XLA Modules:
  0.0 74.8 jit_solution(3360749453162942571)
XLA Ops:
  0.0 72.5 %shard_map.91 = bf16[2048,256]{1,0:T(8,128)(2,1)} custom-call(bf16[2048,256]{1,0:T(8,128)(2,1)} %feats_in.1, bf16[256,256]{1,0:T(8,128)(2,1)} %w_query_in.1, bf16[256,256]{1,0:T(8,128)(2,1)} %w_key_in.1, bf16[256,256]{1,0:T(8,128)(2,1)} %w_value_in.1, bf16[256,256]{1,0:T(8,128)(2,1)} %w_graph_in.1, s32[1,1,16,256]{3,2,1,0:T(8,128)} %src_in.1, ...), custom_call_target="tpu_custom_call" | custom-call | tf_op jit(solution)/shard_map/pallas_call | solution.py:295
  72.5 2.3 %copy.11 = bf16[2048,256]{1,0:T(8,128)(2,1)} copy(bf16[2048,256]{1,0:T(8,128)(2,1)} %shard_map.91) | data formatting | bytes 2097152

commit v4 on v3

--- a/solution.py
+++ b/solution.py
@@ -23,6 +23,7 @@
     outgoing, incoming, src_hi, src_lo, acc, attn, q_hi, q_lo,
     kv_local, kv_parts, kv_plane, kv_columns, kv_total,
     load_sem, edge_send, edge_recv, part_send, part_recv, column_send, column_recv, total_send, total_recv,
+    back_send, back_recv,
 ):
     total = nodes * groups
     plane = inner * groups
@@ -31,6 +32,8 @@
     slots = src_index.shape[3]
     blocks = rows // BLK
     chunk = width // plane
+    sub = chunk // outer
+    halved = sub % 8 == 0
     node = lax.axis_index("node")
     group = lax.axis_index("group")
     me = node * groups + group
@@ -157,10 +160,25 @@
 
     def column_copy(j):
         return pltpu.make_async_remote_copy(
-            src_ref=kv_plane, dst_ref=kv_columns.at[j - 1],
+            src_ref=kv_plane.at[pl.ds(lax.rem(level + j, outer) * sub, sub)] if halved else kv_plane,
+            dst_ref=kv_columns.at[j - 1, pl.ds(0, sub)] if halved else kv_columns.at[j - 1],
             send_sem=column_send.at[j], recv_sem=column_recv.at[j],
             device_id=(lax.rem(node + j * inner, nodes), group), device_id_type=MESH,
         )
+
+    def back_copy(j):
+        own = kv_total.at[spot, pl.ds(level * sub, sub)]
+        return pltpu.make_async_remote_copy(
+            src_ref=own, dst_ref=own, send_sem=back_send.at[j], recv_sem=back_recv.at[j],
+            device_id=(lax.rem(node + j * inner, nodes), group), device_id_type=MESH,
+        )
+
+    def start_back():
+        if halved:
+            each(1, outer, lambda j: column_copy(j).wait_recv())
+            at = pl.ds(pl.multiple_of(level * sub, 8), sub)
+            kv_total[spot, at, :] = kv_plane[at, :] + jnp.sum(kv_columns[:, 0:sub, :], axis=0)
+            each(1, outer, lambda j: back_copy(j).start())
 
     def total_copy(j):
         peer, device = place(j)
@@ -186,8 +204,11 @@
         each(1, outer, lambda j: column_copy(j).start())
 
     def start_totals():
-        each(1, outer, lambda j: column_copy(j).wait_recv())
-        kv_total[spot] = kv_plane[...] + jnp.sum(kv_columns[...], axis=0)
+        if halved:
+            each(1, outer, lambda j: back_copy(j).wait_recv())
+        else:
+            each(1, outer, lambda j: column_copy(j).wait_recv())
+            kv_total[spot] = kv_plane[...] + jnp.sum(kv_columns[...], axis=0)
         each(1, plane, lambda j: total_copy(j).start())
 
     def wait_totals():
@@ -261,9 +282,11 @@
     start_parts()
     lax.fori_loop(5, 8, send_edges, 0)
     start_columns()
-    lax.fori_loop(8, 12, send_edges, 0)
+    lax.fori_loop(8, 11, send_edges, 0)
+    start_back()
+    lax.fori_loop(11, 14, send_edges, 0)
     start_totals()
-    lax.fori_loop(12, nodes, send_edges, 0)
+    lax.fori_loop(14, nodes, send_edges, 0)
     pick(node, incoming.at[0])
     first_batch()
     lax.fori_loop(1, nodes // batch - 1, rest, 0)
@@ -282,6 +305,8 @@
     each(1, plane, lambda j: part_copy(j).wait_send())
     each(1, outer, lambda j: column_copy(j).wait_send())
     each(1, plane, lambda j: total_copy(j).wait_send())
+    if halved:
+        each(1, outer, lambda j: back_copy(j).wait_send())
 
 
 def body(nodes, groups, *arrays):
@@ -321,6 +346,8 @@
             pltpu.SemaphoreType.DMA((nodes // inner,)),
             pltpu.SemaphoreType.DMA((plane,)),
             pltpu.SemaphoreType.DMA,
+            pltpu.SemaphoreType.DMA((nodes // inner,)),
+            pltpu.SemaphoreType.DMA((nodes // inner,)),
         ],
         compiler_params=pltpu.CompilerParams(
             collective_id=0, has_side_effects=True, vmem_limit_bytes=62 * 1024 * 1024

time: 75 us -> 76.9 us (1.025); the launches traced: 74.8 us -> 75.5 us
  no operation moved by 1% of the time
where the time goes in v4:
time: 76.9 us; the launch traced here: 75.5 us
  Pallas kernels  73.2 us (95%)
  local copies, waits for them, and re-layouts  2.26 us (3%)
    pallas_call x1, Pallas kernels, body(): pl.pallas_call(functools.partial(kernel, nodes, groups, inner, 4), out_sh...  73.2 us
    unnamed x1, local copies, waits for them, and re-layouts  2.26 us

profile of v4, /device:TPU:27, one launch (start us, length us, event | category | flops | bytes accessed | tf_op | source)
XLA Modules:
  0.0 75.5 jit_solution(10205979844631900552)
XLA Ops:
  0.0 73.2 %shard_map.91 = bf16[2048,256]{1,0:T(8,128)(2,1)} custom-call(bf16[2048,256]{1,0:T(8,128)(2,1)} %feats_in.1, bf16[256,256]{1,0:T(8,128)(2,1)} %w_query_in.1, bf16[256,256]{1,0:T(8,128)(2,1)} %w_key_in.1, bf16[256,256]{1,0:T(8,128)(2,1)} %w_value_in.1, bf16[256,256]{1,0:T(8,128)(2,1)} %w_graph_in.1, s32[1,1,16,256]{3,2,1,0:T(8,128)} %src_in.1, ...), custom_call_target="tpu_custom_call" | custom-call | tf_op jit(solution)/shard_map/pallas_call | solution.py:320
  73.2 2.3 %copy.11 = bf16[2048,256]{1,0:T(8,128)(2,1)} copy(bf16[2048,256]{1,0:T(8,128)(2,1)} %shard_map.91) | data formatting | bytes 2097152
